TPU v7x, 32 devices: a whole 2x2x4 slice. The times are simulated.
32 devices in a mesh: parts: 1, ctx: 4 (over z), pb: 4 (over y, x), row: 2 (over core).
Axes of the slice: x: 2, y: 2, z: 4, core: 2. Of those that a mesh axis runs over, the one named last changes fastest.
Arguments:
- queries: bfloat16 [2048, 3072], P(('parts', 'ctx', 'pb', 'row')), may hold values from -10 to 10
- cache_keys: bfloat16 [4096, 192], P(('parts', 'ctx')), may hold values from -10 to 10
- cache_values: bfloat16 [4096, 128], P(('parts', 'ctx')), may hold values from -6 to 6
- span_keys: bfloat16 [2048, 192], P(('parts', 'ctx')), may hold values from -10 to 10
- span_values: bfloat16 [2048, 128], P(('parts', 'ctx')), may hold values from -6 to 6
- pool_keys: float32 [32, 192], replicated, may hold values from 0.2 to 0.6
- pool_values: float32 [32, 128], replicated, may hold values from 0.05 to 0.3
- gate_logits: bfloat16 [2048, 48], P(('parts', 'ctx', 'pb', 'row')), may hold values from -6 to 6
- chosen_blocks: int32 [32, 16], P(('parts', 'ctx', 'pb', 'row')), may hold values from 0 to 95, as said below
- valid_counts: int32 [32], P(('parts', 'ctx', 'pb', 'row')), may hold values from 4 to 16
Outputs:
- mixed: bfloat16 [2048, 2048], P(('parts', 'ctx', 'pb', 'row'))
Inputs may be any that keep to these rules, and one draw needn't show every extreme that they name: `chosen_blocks`: slot 0 of tile t holds the tile's own block 64 + t. Slot s > 0 holds a block of the cache stored by ctx index (c + s) mod (4), where c is the ctx index that holds tile t; the blocks of one tile are distinct. Slots at or beyond the tile's valid count hold blocks too and are ignored.
All inputs are finite; a program needn't handle non-finite values.
Results may differ from a plain program's by a relative error of at most 0.0034.
The roundings to bfloat16 on the way count: a program that leaves them out, or rounds other values in their place, can miss the bound.
Values may be sent and summed in bfloat16 or wider, within the bound.
A program may use at most 64 MiB of HBM per device.

v0:
```python
import math
import jax
import jax.numpy as jnp
from jax import lax
from jax.sharding import PartitionSpec as P

HEADS = 16
CLEN = 32
STRIDE = 16
BLOCK = 64
WINDOW = 256
NEG_FILL = -1e30


def from_behind(value, axis, steps):
    count = lax.axis_size(axis)
    pairs = [(source, (source + steps) % count) for source in range(count)]
    return lax.ppermute(value, axis, pairs)


def pool_blocks(rows, extra, weights, stride):
    joined = jnp.concatenate([rows, extra], axis=0).astype(jnp.float32)
    blocks = rows.shape[0] // stride
    grouped = joined.reshape(blocks + 1, stride, rows.shape[1])
    leading = jnp.sum(grouped[:-1] * weights[None, :stride, :], axis=1)
    trailing = jnp.sum(grouped[1:] * weights[None, stride:, :], axis=1)
    return (leading + trailing).astype(jnp.bfloat16)


def attend(query_rows, keys, values, visible, score_scale):
    scores = jnp.dot(query_rows, keys.T, preferred_element_type=jnp.float32) * score_scale
    scores = jnp.where(visible, scores, NEG_FILL)
    highest = jnp.max(scores, axis=1, keepdims=True)
    exponent = jnp.where(visible, jnp.exp(scores - highest), 0.0)
    weights = exponent.astype(jnp.bfloat16)
    numerator = jnp.dot(weights, values, preferred_element_type=jnp.float32)
    return numerator / jnp.sum(exponent, axis=1, keepdims=True)


def local(
    queries,
    cache_keys,
    cache_values,
    span_keys,
    span_values,
    pool_keys,
    pool_values,
    gate_logits,
    chosen_blocks,
    valid_counts,
):
    owners = lax.axis_size("ctx")
    ctx_place = lax.axis_index("ctx")
    tile_place = lax.axis_index("pb") * lax.axis_size("row") + lax.axis_index("row")
    cache_len, key_width = cache_keys.shape
    value_width = cache_values.shape[1]
    span_len = span_keys.shape[0]
    tokens = queries.shape[0]
    tiles_here = chosen_blocks.shape[0]
    score_scale = 1.0 / math.sqrt(key_width)
    context_start = cache_len * owners
    local_start = tile_place * tokens
    first_pos = context_start + ctx_place * span_len + local_start
    row_count = tokens * HEADS
    query_rows = queries.reshape(row_count, key_width)
    row_pos = first_pos + jnp.arange(row_count, dtype=jnp.int32) // HEADS
    leader = ctx_place == 0
    outgoing = (
        jnp.where(leader, span_keys[:STRIDE], cache_keys[:STRIDE]),
        jnp.where(leader, span_values[:STRIDE], cache_values[:STRIDE]),
        span_keys[:STRIDE],
        span_values[:STRIDE],
    )
    heads_next = from_behind((outgoing[0], outgoing[1], outgoing[2], outgoing[3]), "ctx", -1)
    summary_keys = jnp.concatenate(
        [
            pool_blocks(cache_keys, heads_next[0], pool_keys, STRIDE),
            pool_blocks(span_keys, heads_next[2], pool_keys, STRIDE),
        ],
        axis=0,
    )
    summary_values = jnp.concatenate(
        [
            pool_blocks(cache_values, heads_next[1], pool_values, STRIDE),
            pool_blocks(span_values, heads_next[3], pool_values, STRIDE),
        ],
        axis=0,
    )
    cache_blocks = cache_len // STRIDE
    span_blocks = span_len // STRIDE
    per_ctx = cache_blocks + span_blocks
    first_row = jnp.int32(0)
    running_max = jnp.full((row_count,), NEG_FILL, jnp.float32)
    running_sum = jnp.zeros((row_count,), jnp.float32)
    running_out = jnp.zeros((row_count, value_width), jnp.float32)
    part_keys = lax.all_gather(summary_keys, "ctx", axis=0, tiled=True)
    part_values = lax.all_gather(summary_values, "ctx", axis=0, tiled=True)
    length = part_keys.shape[0]
    for lower_row in range(0, length, 512):
        upper_row = min(lower_row + 512, length)
        block_index = first_row + lower_row + jnp.arange(upper_row - lower_row, dtype=jnp.int32)
        owner_of = block_index // per_ctx
        within = block_index % per_ctx
        block_id = jnp.where(
            within < cache_blocks,
            owner_of * cache_blocks + within,
            owners * cache_blocks + owner_of * span_blocks + within - cache_blocks,
        )
        visible = (block_id * STRIDE + CLEN)[None, :] <= row_pos[:, None] + 1
        scores = (
            jnp.dot(
                query_rows, part_keys[lower_row:upper_row].T, preferred_element_type=jnp.float32
            )
            * score_scale
        )
        scores = jnp.where(visible, scores, NEG_FILL)
        new_max = jnp.maximum(running_max, jnp.max(scores, axis=1))
        exponent = jnp.where(visible, jnp.exp(scores - new_max[:, None]), 0.0)
        fading = jnp.exp(running_max - new_max)
        running_sum = running_sum * fading + jnp.sum(exponent, axis=1)
        running_out = running_out * fading[:, None] + jnp.dot(
            exponent.astype(jnp.bfloat16),
            part_values[lower_row:upper_row],
            preferred_element_type=jnp.float32,
        )
        running_max = new_max
    summary_out = running_out / running_sum[:, None]
    reach = chosen_blocks.shape[1] // owners
    arranged = chosen_blocks.reshape(tiles_here, reach, owners)
    column_of = (jnp.arange(owners, dtype=jnp.int32) - ctx_place) % owners
    requested = jnp.take(arranged, column_of, axis=2)
    wanted = lax.all_to_all(requested, "ctx", split_axis=2, concat_axis=2, tiled=True)
    cache_count = cache_len // BLOCK
    span_count = span_len // BLOCK
    from_cache = (wanted < owners * cache_count)[..., None, None]
    cache_slot = jnp.clip(wanted - ctx_place * cache_count, 0, cache_count - 1)
    span_slot = jnp.clip(wanted - owners * cache_count - ctx_place * span_count, 0, span_count - 1)
    served_keys = jnp.where(
        from_cache,
        cache_keys.reshape(cache_count, BLOCK, key_width)[cache_slot],
        span_keys.reshape(span_count, BLOCK, key_width)[span_slot],
    )
    served_values = jnp.where(
        from_cache,
        cache_values.reshape(cache_count, BLOCK, value_width)[cache_slot],
        span_values.reshape(span_count, BLOCK, value_width)[span_slot],
    )
    fetched_keys, fetched_values = (
        lax.all_to_all(served_keys, "ctx", split_axis=2, concat_axis=2, tiled=True),
        lax.all_to_all(served_values, "ctx", split_axis=2, concat_axis=2, tiled=True),
    )
    last_ctx = ctx_place == owners - 1
    tail_rows = from_behind(
        (
            jnp.where(last_ctx, cache_keys[-WINDOW:], span_keys[-WINDOW:]),
            jnp.where(last_ctx, cache_values[-WINDOW:], span_values[-WINDOW:]),
        ),
        "ctx",
        1,
    )
    reach_keys = jnp.concatenate([tail_rows[0], span_keys], axis=0)
    reach_values = jnp.concatenate([tail_rows[1], span_values], axis=0)
    gate_values = jax.nn.sigmoid(gate_logits.astype(jnp.float32)).reshape(tokens, 3, HEADS)
    offsets = jnp.arange(BLOCK, dtype=jnp.int32)
    near_offsets = jnp.arange(WINDOW + BLOCK, dtype=jnp.int32)
    slot_number = jnp.arange(reach, dtype=jnp.int32)[:, None] * owners + column_of[None, :]
    key_pos = (requested[0][:, :, None] * BLOCK + offsets).reshape(-1)
    usable = jnp.repeat((slot_number < valid_counts[0]).reshape(-1), BLOCK)
    sel_visible = usable[None, :] & (key_pos[None, :] <= row_pos[:, None])
    picked = attend(
        query_rows,
        fetched_keys[0].reshape(-1, key_width),
        fetched_values[0].reshape(-1, value_width),
        sel_visible,
        score_scale,
    )
    begin = local_start + 0
    near_keys = lax.dynamic_slice_in_dim(reach_keys, begin, WINDOW + BLOCK, 0)
    near_values = lax.dynamic_slice_in_dim(reach_values, begin, WINDOW + BLOCK, 0)
    near_pos = context_start + ctx_place * span_len - WINDOW + begin + near_offsets
    near_visible = (near_pos[None, :] <= row_pos[:, None]) & (
        near_pos[None, :] > row_pos[:, None] - WINDOW
    )
    nearby = attend(query_rows, near_keys, near_values, near_visible, score_scale)
    mixed = (
        gate_values[:, 0, :, None] * summary_out.reshape(BLOCK, HEADS, value_width)
        + gate_values[:, 1, :, None] * picked.reshape(BLOCK, HEADS, value_width)
        + gate_values[:, 2, :, None] * nearby.reshape(BLOCK, HEADS, value_width)
    )
    outputs = mixed.reshape(BLOCK, HEADS * value_width).astype(jnp.bfloat16)
    return outputs


def solution(mesh):
    return jax.shard_map(
        local,
        mesh=mesh,
        in_specs=(
            P(("parts", "ctx", "pb", "row"), None),
            P(("parts", "ctx"), None),
            P(("parts", "ctx"), None),
            P(("parts", "ctx"), None),
            P(("parts", "ctx"), None),
            P(),
            P(),
            P(("parts", "ctx", "pb", "row"), None),
            P(("parts", "ctx", "pb", "row"), None),
            P(("parts", "ctx", "pb", "row")),
        ),
        out_specs=P(("parts", "ctx", "pb", "row"), None),
        check_vma=False,
    )
```

profile of v0, /device:TPU:0, one launch (start us, length us, event | category | flops | bytes accessed | tf_op | source)
XLA Modules:
  0.0 91.8 jit_solution(5316688061465802636)
XLA Ops:
  0.0 1.3 %copy.79 = bf16[1024,192]{1,0:T(8,128)(2,1)S(1)} copy(bf16[1024,192]{0,1:T(8,128)(2,1)} %param.11) | data formatting | bytes 786432 | tf_op args[1]
  1.3 1.1 %copy.77 = bf16[512,192]{1,0:T(8,128)(2,1)S(1)} copy(bf16[512,192]{0,1:T(8,128)(2,1)} %param.13) | data formatting | bytes 393216 | tf_op args[3]
  2.4 0.6 slice_select_fusion.2
  3.0 5.1 %collective-permute-start = (bf16[16,192]{1,0:T(8,128)(2,1)}, bf16[16,192]{1,0:T(8,128)(2,1)}, u32[]{:S(2)}, u32[]{:S(2)}) collective-permute-start(bf16[16,192]{1,0:T(8,128)(2,1)} %get-tuple-element.13), channel_id=1, source_target_pairs={{0,24},{8,0},{16,8},{24,16},{1,25},{9,1},{17,9},{25,17},{2,26},{10... | collective-permute-start | bytes 18440 | tf_op jit(solution)/shard_map/ppermute | solution.py:18
  8.0 0.4 collective-permute-start.1
  8.5 1.3 %slice_select_fusion.3 = (bf16[16,128]{1,0:T(8,128)(2,1)}, bf16[16,128]{1,0:T(8,128)(2,1)}) fusion(bf16[1024,128]{1,0:T(8,128)(2,1)} %param.12, pred[]{:T(512)S(6)} %eq.10, bf16[512,128]{1,0:T(8,128)(2,1)} %param.14), kind=kLoop, calls=%fused_computation.87 | loop fusion | flops 2048 | bytes 16385 | tf_op jit(solution)/shard_map/jit(_where)/select_n | solution.py:70
  9.8 0.4 collective-permute-start.2
  10.3 0.5 broadcast.494
  10.8 1.3 %reduce.3 = s32[16]{0:T(128)S(1)} reduce(s32[1,16]{1,0:T(1,128)} %param.18, s32[]{:T(128)} %broadcast.494), dimensions={0}, to_apply=%param.18.reduce_sub_computation.3 | reduce | bytes 132 | tf_op args[8]
  12.2 0.1 copy.82
  12.3 0.6 gather_fusion
  12.9 0.1 copy.84
  13.0 0.7 copy.85
  13.7 5.3 %all-to-all-start = ((s32[1,4,4]{1,0,2:T(1,128)}), s32[1,4,4]{1,0,2:T(1,128)S(1)}, u32[]{:S(2)}, u32[]{:S(2)}) async-start(s32[1,4,4]{1,0,2:T(1,128)} %copy.85), calls=%async_computation | async-start | bytes 4096 | tf_op jit(solution)/shard_map/all_to_all | solution.py:132
  18.9 1.0 %slice_select_fusion = bf16[256,192]{0,1:T(8,128)(2,1)S(1)} fusion(bf16[512,192]{0,1:T(8,128)(2,1)} %param.13, bf16[1024,192]{0,1:T(8,128)(2,1)} %param.11, pred[]{:T(512)S(6)} %eq.11), kind=kLoop, calls=%fused_computation.60 | loop fusion | flops 49152 | bytes 294913 | tf_op jit(solution)/shard_map/jit(_where)/select_n | solution.py:155
  19.9 2.1 %collective-permute-start.4 = (bf16[256,192]{0,1:T(8,128)(2,1)S(1)}, bf16[256,192]{0,1:T(8,128)(2,1)}, u32[]{:S(2)}, u32[]{:S(2)}) collective-permute-start(bf16[256,192]{0,1:T(8,128)(2,1)S(1)} %slice_select_fusion), channel_id=1, source_target_pairs={{0,8},{8,16},{16,24},{24,0},{1,9},{9,17},{17,25},{25,1},{2,10},{10... | collective-permute-start | bytes 294920 | tf_op jit(solution)/shard_map/ppermute | solution.py:18
  22.0 0.6 multiply_add_fusion
  22.8 0.6 reshape.297
  23.4 0.1 copy.83
  24.4 0.1 lt.66
  24.5 0.6 and.99
  25.2 0.7 copy.76
  25.9 0.7 copy.81
  26.6 0.7 copy.97
  27.3 0.1 copy.89
  27.5 0.1 copy.91
  27.6 0.1 copy.86
  27.7 0.1 copy.87
  27.9 0.6 gather_fusion.1
  28.4 0.6 gather_fusion.3
  29.1 0.6 gather_fusion.2
  29.6 0.6 gather_fusion.4
  30.2 0.1 broadcast_select_fusion
  30.3 0.7 copy.95
  31.1 3.6 %all-to-all-start.2 = ((bf16[1,4,4,64,128]{4,3,1,0,2:T(8,128)(2,1)}), bf16[1,4,4,64,128]{4,3,1,0,2:T(8,128)(2,1)S(1)}, u32[]{:S(2)}, u32[]{:S(2)}) async-start(bf16[1,4,4,64,128]{4,3,1,0,2:T(8,128)(2,1)} %copy.95), calls=%async_computation.2 | async-start | bytes 524288 | tf_op jit(solution)/shard_map/all_to_all | solution.py:150
  34.7 0.9 copy_select_fusion
  35.6 2.0 %collective-permute-start.5 = (bf16[256,128]{1,0:T(8,128)(2,1)S(1)}, bf16[256,128]{1,0:T(8,128)(2,1)}, u32[]{:S(2)}, u32[]{:S(2)}) collective-permute-start(bf16[256,128]{1,0:T(8,128)(2,1)S(1)} %slice_select_fusion.1), channel_id=1, source_target_pairs={{0,8},{8,16},{16,24},{24,0},{1,9},{9,17},{17,25},{25,1},{2,10},{10... | collective-permute-start | bytes 196616 | tf_op jit(solution)/shard_map/ppermute | solution.py:18
  37.6 0.7 maximum_convert_fusion.2
  38.4 0.7 maximum_convert_fusion.3
  39.2 0.2 multiply_reduce_fusion.2
  39.4 0.1 multiply_reduce_fusion.6
  39.6 13.2 %all_gather.7 = bf16[384,128]{1,0:T(8,128)(2,1)S(1)} all-gather(bf16[96,128]{1,0:T(8,128)(2,1)S(1)} %pad_maximum_fusion.1), channel_id=1, replica_groups=mesh['parts'=1,'ctx'=4,'pb'=4,'row'=2] {'ctx'}, dimensions={0}, use_global_device_ids=true | all-gather | bytes 122880 | tf_op jit(solution)/shard_map/all_gather | solution.py:97
  52.8 0.8 maximum_convert_fusion
  53.6 0.2 fusion.53
  53.8 0.7 maximum_convert_fusion.1
  54.6 0.5 multiply_reduce_fusion
  55.2 0.3 multiply_reduce_fusion.4
  55.5 13.6 %all_gather.6 = bf16[384,192]{1,0:T(8,128)(2,1)S(1)} all-gather(bf16[96,192]{1,0:T(8,128)(2,1)S(1)} %pad_maximum_fusion), channel_id=1, replica_groups=mesh['parts'=1,'ctx'=4,'pb'=4,'row'=2] {'ctx'}, dimensions={0}, use_global_device_ids=true | all-gather | bytes 184320 | tf_op jit(solution)/shard_map/all_gather | solution.py:96
  69.0 0.4 fusion.60
  69.5 0.3 fusion.9
  69.8 0.7 fusion.5
  70.6 3.7 %all-to-all-start.1 = ((bf16[1,4,4,64,192]{4,3,1,0,2:T(8,128)(2,1)}), bf16[1,4,4,64,192]{4,3,1,0,2:T(8,128)(2,1)S(1)}, u32[]{:S(2)}, u32[]{:S(2)}) async-start(bf16[1,4,4,64,192]{4,3,1,0,2:T(8,128)(2,1)} %copy_select_fusion), calls=%async_computation.1 | async-start | bytes 1048576 | tf_op jit(solution)/shard_map/all_to_all | solution.py:149
  74.3 1.7 %fusion.59 = (f32[1024]{0:T(1024)S(1)}, f32[1024,320]{0,1:T(8,128)S(1)}) fusion(bf16[1024,192]{1,0:T(8,128)(2,1)S(1)} %reshape.297, s32[]{:T(128)S(6)} %select_n.211, bf16[256,192]{0,1:T(8,128)(2,1)} %collective-permute-done.4, bf16[512,192]{0,1:T(8,128)(2,1)S(1)} %copy-done.2, s32[1024]{0:T(1024)S(1)} %broadcast_add_fusion, s32[1024]{0:T(1024)S(1)} %fusion.31, ...), kind=kOutput, calls=%fused_computation.137 | convolution fusion | flops 128039936 | bytes 2012420 | tf_op jit(solution)/shard_map/dot_general | solution.py:31
  76.0 0.4 fusion.11
  76.4 1.5 %convolution_divide_fusion = f32[1024,128]{1,0:T(8,128)S(1)} fusion(f32[1024,320]{0,1:T(8,128)S(1)} %get-tuple-element.29, f32[1024]{0:T(1024)S(1)} %get-tuple-element.28, s32[1024]{0:T(1024)S(1)} %broadcast_add_fusion, s32[1024]{0:T(1024)S(1)} %fusion.31, s32[320]{0:T(512)S(1)} %iota_add_fusion.1, f32[1024]{0:T(1024)S(1)} %fusion.11, s32[]{:T(128)S(6)} %select_n.211, ...), kind=kOutput, calls=%fused_computation.21 | convolution fusion | flops 86147072 | bytes 2049284 | tf_op jit(solution)/shard_map/dot_general | solution.py:36
  78.0 6.4 %all-to-all-done.1 = bf16[1,4,4,64,192]{4,3,1,0,2:T(8,128)(2,1)S(1)} async-done(((bf16[1,4,4,64,192]{4,3,1,0,2:T(8,128)(2,1)}), bf16[1,4,4,64,192]{4,3,1,0,2:T(8,128)(2,1)S(1)}, u32[]{:S(2)}, u32[]{:S(2)}) %all-to-all-start.1) | async-done | bytes 393248 | tf_op jit(solution)/shard_map/all_to_all | solution.py:149
  84.4 1.2 %fusion = (f32[1024]{0:T(1024)S(1)}, f32[1024,1024]{1,0:T(8,128)S(1)}) fusion(s32[1024]{0:T(1024)S(1)} %fusion.31, s32[1024]{0:T(1024)S(1)} %add.265, pred[1024]{0:T(1024)(128)(4,1)S(1)} %copy-done.11, bf16[1024,192]{1,0:T(8,128)(2,1)S(1)} %bitcast.97, bf16[1024,192]{1,0:T(8,128)(2,1)S(1)} %reshape.297), kind=kOutput, calls=%fused_computation.8 | convolution fusion | flops 407895040 | bytes 4994048 | tf_op jit(solution)/shard_map/dot_general | solution.py:31
  85.6 1.9 %fusion.52 = f32[1024]{0:T(1024)S(1)} fusion(f32[1024]{0:T(1024)S(1)} %get-tuple-element.30, f32[1024,1024]{1,0:T(8,128)S(1)} %get-tuple-element.31, s32[1024]{0:T(1024)S(1)} %fusion.31, s32[1024]{0:T(1024)S(1)} %add.265, pred[1024]{0:T(1024)(128)(4,1)S(1)} %copy-done.11), kind=kLoop, calls=%fused_computation.130 | loop fusion | flops 7339008 | bytes 4211712 | tf_op jit(solution)/shard_map/reduce_sum | solution.py:37
  87.5 1.8 %fusion.6 = f32[1024,128]{1,0:T(8,128)S(1)} fusion(bf16[1024,128]{1,0:T(8,128)(2,1)S(1)} %bitcast.98, f32[1024]{0:T(1024)S(1)} %fusion.52, f32[1024,1024]{1,0:T(8,128)S(1)} %get-tuple-element.31, f32[1024]{0:T(1024)S(1)} %get-tuple-element.30, s32[1024]{0:T(1024)S(1)} %fusion.31, s32[1024]{0:T(1024)S(1)} %add.265, pred[1024]{0:T(1024)(128)(4,1)S(1)} %copy-done.11), kind=kOutput, calls=%fused_computation.20 | convolution fusion | flops 275906560 | bytes 4998144 | tf_op jit(solution)/shard_map/dot_general | solution.py:36
  89.5 0.2 mul.192
  89.7 0.4 copy-done.5
  90.2 0.2 mul.223
  90.4 0.2 mul.234
  90.6 1.3 %fusion.25 = bf16[64,2048]{1,0:T(8,128)(2,1)} fusion(f32[64,2048]{1,0:T(8,128)S(1)} %reshape.305, f32[8,8,16,128]{3,2,1,0:T(8,128)S(1)} %bitcast.92, f32[64,2048]{1,0:T(8,128)S(1)} %reshape.304, f32[8,8,16,128]{3,2,1,0:T(8,128)S(1)} %bitcast.91, f32[64,2048]{1,0:T(8,128)S(1)} %reshape.298, f32[8,8,16,128]{3,2,1,0:T(8,128)S(1)} %bitcast.90), kind=kLoop, calls=%fused_computation.40 | loop fusion | flops 786432 | bytes 3407872 | tf_op jit(solution)/shard_map/convert_element_type | solution.py:190
  (75 shorter events, 1.4 us)
Async XLA Ops:
  0.0 22.7 %copy-start.1 = (bf16[1024,128]{1,0:T(8,128)(2,1)S(1)}, bf16[1024,128]{1,0:T(8,128)(2,1)}, u32[]{:S(2)}) copy-start(bf16[1024,128]{1,0:T(8,128)(2,1)} %param.12) | copy-start | bytes 786436
  0.0 22.7 %copy-start = (bf16[512,128]{1,0:T(8,128)(2,1)S(1)}, bf16[512,128]{1,0:T(8,128)(2,1)}, u32[]{:S(2)}) copy-start(bf16[512,128]{1,0:T(8,128)(2,1)} %param.14) | copy-start | bytes 393220
  0.0 22.7 %copy-start.7 = (f32[32,192]{1,0:T(8,128)S(1)}, f32[32,192]{1,0:T(8,128)}, u32[]{:S(2)}) copy-start(f32[32,192]{1,0:T(8,128)} %param.15) | copy-start | bytes 73732
  0.0 22.7 %copy-start.3 = (bf16[64,3072]{1,0:T(8,128)(2,1)S(1)}, bf16[64,3072]{1,0:T(8,128)(2,1)}, u32[]{:S(2)}) copy-start(bf16[64,3072]{1,0:T(8,128)(2,1)} %param.10) | copy-start | bytes 1179652
  0.0 23.4 %copy-start.8 = (f32[32,128]{1,0:T(8,128)S(1)}, f32[32,128]{1,0:T(8,128)}, u32[]{:S(2)}) copy-start(f32[32,128]{1,0:T(8,128)} %param.16) | copy-start | bytes 49156
  0.0 25.2 %copy-start.9 = (bf16[64,48]{0,1:T(8,128)(2,1)S(1)}, bf16[64,48]{0,1:T(8,128)(2,1)}, u32[]{:S(2)}) copy-start(bf16[64,48]{0,1:T(8,128)(2,1)} %param.17) | copy-start | bytes 18436
  3.0 49.8 %collective-permute-start = (bf16[16,192]{1,0:T(8,128)(2,1)}, bf16[16,192]{1,0:T(8,128)(2,1)}, u32[]{:S(2)}, u32[]{:S(2)}) collective-permute-start(bf16[16,192]{1,0:T(8,128)(2,1)} %get-tuple-element.13), channel_id=1, source_target_pairs={{0,24},{8,0},{16,8},{24,16},{1,25},{9,1},{17,9},{25,17},{2,26},{10... | collective-permute-start | bytes 18440 | tf_op jit(solution)/shard_map/ppermute | solution.py:18
  8.0 45.7 %collective-permute-start.1 = (bf16[16,192]{1,0:T(8,128)(2,1)}, bf16[16,192]{1,0:T(8,128)(2,1)}, u32[]{:S(2)}, u32[]{:S(2)}) collective-permute-start(bf16[16,192]{1,0:T(8,128)(2,1)} %get-tuple-element.14), channel_id=1, source_target_pairs={{0,24},{8,0},{16,8},{24,16},{1,25},{9,1},{17,9},{25,17},{2,26},{10... | collective-permute-start | bytes 18440 | tf_op jit(solution)/shard_map/ppermute | solution.py:18
  9.8 25.8 %collective-permute-start.2 = (bf16[16,128]{1,0:T(8,128)(2,1)}, bf16[16,128]{1,0:T(8,128)(2,1)}, u32[]{:S(2)}, u32[]{:S(2)}) collective-permute-start(bf16[16,128]{1,0:T(8,128)(2,1)} %get-tuple-element.15), channel_id=1, source_target_pairs={{0,24},{8,0},{16,8},{24,16},{1,25},{9,1},{17,9},{25,17},{2,26},{10... | collective-permute-start | bytes 12296 | tf_op jit(solution)/shard_map/ppermute | solution.py:18
  10.2 28.2 %collective-permute-start.3 = (bf16[16,128]{1,0:T(8,128)(2,1)}, bf16[16,128]{1,0:T(8,128)(2,1)}, u32[]{:S(2)}, u32[]{:S(2)}) collective-permute-start(bf16[16,128]{1,0:T(8,128)(2,1)} %get-tuple-element.16), channel_id=1, source_target_pairs={{0,24},{8,0},{16,8},{24,16},{1,25},{9,1},{17,9},{25,17},{2,26},{10... | collective-permute-start | bytes 12296 | tf_op jit(solution)/shard_map/ppermute | solution.py:18
  13.7 13.6 %all-to-all-start = ((s32[1,4,4]{1,0,2:T(1,128)}), s32[1,4,4]{1,0,2:T(1,128)S(1)}, u32[]{:S(2)}, u32[]{:S(2)}) async-start(s32[1,4,4]{1,0,2:T(1,128)} %copy.85), calls=%async_computation | async-start | bytes 4096 | tf_op jit(solution)/shard_map/all_to_all | solution.py:132
  19.9 54.4 %collective-permute-start.4 = (bf16[256,192]{0,1:T(8,128)(2,1)S(1)}, bf16[256,192]{0,1:T(8,128)(2,1)}, u32[]{:S(2)}, u32[]{:S(2)}) collective-permute-start(bf16[256,192]{0,1:T(8,128)(2,1)S(1)} %slice_select_fusion), channel_id=1, source_target_pairs={{0,8},{8,16},{16,24},{24,0},{1,9},{9,17},{17,25},{25,1},{2,10},{10... | collective-permute-start | bytes 294920 | tf_op jit(solution)/shard_map/ppermute | solution.py:18
  31.1 39.6 %all-to-all-start.2 = ((bf16[1,4,4,64,128]{4,3,1,0,2:T(8,128)(2,1)}), bf16[1,4,4,64,128]{4,3,1,0,2:T(8,128)(2,1)S(1)}, u32[]{:S(2)}, u32[]{:S(2)}) async-start(bf16[1,4,4,64,128]{4,3,1,0,2:T(8,128)(2,1)} %copy.95), calls=%async_computation.2 | async-start | bytes 524288 | tf_op jit(solution)/shard_map/all_to_all | solution.py:150
  35.6 40.8 %collective-permute-start.5 = (bf16[256,128]{1,0:T(8,128)(2,1)S(1)}, bf16[256,128]{1,0:T(8,128)(2,1)}, u32[]{:S(2)}, u32[]{:S(2)}) collective-permute-start(bf16[256,128]{1,0:T(8,128)(2,1)S(1)} %slice_select_fusion.1), channel_id=1, source_target_pairs={{0,8},{8,16},{16,24},{24,0},{1,9},{9,17},{17,25},{25,1},{2,10},{10... | collective-permute-start | bytes 196616 | tf_op jit(solution)/shard_map/ppermute | solution.py:18
  54.6 14.4 %copy-start.10 = (s32[384]{0:T(512)S(1)}, s32[384]{0:T(512)}, u32[]{:S(2)}) copy-start(s32[384]{0:T(512)} %multiply_add_fusion) | copy-start | bytes 4612
  70.5 3.8 %copy-start.2 = (bf16[512,192]{0,1:T(8,128)(2,1)S(1)}, bf16[512,192]{0,1:T(8,128)(2,1)}, u32[]{:S(2)}) copy-start(bf16[512,192]{0,1:T(8,128)(2,1)} %param.13) | copy-start | bytes 589828
  70.6 13.7 %all-to-all-start.1 = ((bf16[1,4,4,64,192]{4,3,1,0,2:T(8,128)(2,1)}), bf16[1,4,4,64,192]{4,3,1,0,2:T(8,128)(2,1)S(1)}, u32[]{:S(2)}, u32[]{:S(2)}) async-start(bf16[1,4,4,64,192]{4,3,1,0,2:T(8,128)(2,1)} %copy_select_fusion), calls=%async_computation.1 | async-start | bytes 1048576 | tf_op jit(solution)/shard_map/all_to_all | solution.py:149
  77.9 6.5 %copy-start.11 = (pred[1024]{0:T(1024)(128)(4,1)S(1)}, pred[1024]{0:T(1024)(128)(4,1)}, u32[]{:S(2)}) copy-start(pred[1024]{0:T(1024)(128)(4,1)} %and.99) | copy-start | bytes 3076
  87.5 2.0 %copy-start.4 = (f32[64,16]{1,0:T(8,128)S(1)}, f32[64,16]{1,0:T(8,128)}, u32[]{:S(2)}) copy-start(f32[64,16]{1,0:T(8,128)} %copy.76) | copy-start | bytes 12292
  89.4 0.8 copy-start.5
  89.4 0.9 %copy-start.6 = (f32[64,16]{1,0:T(8,128)S(1)}, f32[64,16]{1,0:T(8,128)}, u32[]{:S(2)}) copy-start(f32[64,16]{1,0:T(8,128)} %copy.97) | copy-start | bytes 12292
where the time goes:
time: 92.6 us; the launch traced here: 91.8 us
  blocking collectives  26.8 us (29%)
  starting transfers between devices  22.7 us (25%)
  other arithmetic  14.1 us (15%)
  local copies, waits for them, and re-layouts  13.3 us (14%)
  matrix products  7.31 us (8%)
  waiting for transfers between devices  6.38 us (7%)
  between operations  1.25 us (1%)
    all_gather x1, blocking collectives, local(): part_keys = lax.all_gather(summary_keys, 'ctx', axis=0, tiled=True)  13.6 us
    all_gather x1, blocking collectives, local(): part_values = lax.all_gather(summary_values, 'ctx', axis=0, tiled=True)  13.2 us
    ppermute x6, starting transfers between devices, from_behind(): return lax.ppermute(value, axis, pairs)  10.1 us
    all_to_all x1, waiting for transfers between devices, local(): lax.all_to_all(served_keys, 'ctx', split_axis=2, concat_axis=2, tiled=True)  6.36 us
    all_to_all x1, starting transfers between devices, local(): lax.all_to_all(requested, 'ctx', split_axis=2, concat_axis=2, tiled=True)  5.27 us
    all_to_all x1, starting transfers between devices, local(): lax.all_to_all(served_keys, 'ctx', split_axis=2, concat_axis=2, tiled=True)  3.66 us
    all_to_all x1, starting transfers between devices, local(): lax.all_to_all(served_values, 'ctx', split_axis=2, concat_axis=2, tiled=T...  3.63 us
    unnamed x27, local copies, waits for them, and re-layouts  3.33 us
  transfers between devices with their start and end apart: 9, of which 1 were waited for; matrix products, arithmetic and copies ran while one was open for 27% of the time, Pallas kernels for 0%

commit v1 on v0

--- a/solution.py
+++ b/solution.py
@@ -129,7 +129,10 @@
     arranged = chosen_blocks.reshape(tiles_here, reach, owners)
     column_of = (jnp.arange(owners, dtype=jnp.int32) - ctx_place) % owners
     requested = jnp.take(arranged, column_of, axis=2)
-    wanted = lax.all_to_all(requested, "ctx", split_axis=2, concat_axis=2, tiled=True)
+    wanted = jnp.concatenate(
+        lax.all_to_all(jnp.stack(jnp.split(requested, lax.axis_size("ctx"), axis=2)), "ctx", 0, 0),
+        axis=2,
+    )
     cache_count = cache_len // BLOCK
     span_count = span_len // BLOCK
     from_cache = (wanted < owners * cache_count)[..., None, None]

time: 92.6 us -> 98.8 us (1.067)
  other arithmetic: 14.1 us -> 19.6 us
    lt x0 -> x2, local copies, waits for them, and re-layouts: none -> 1.27 us  [local(): from_cache = (wanted < owners * cache_count)[..., None, None]]
    unnamed x27 -> x39, local copies, waits for them, and re-layouts: 3.33 us -> 3.38 us
  transfers between devices with their start and end apart: 9 -> 9, of which waited for: 1 -> 1; matrix products, arithmetic and copies ran while one was open for 27% -> 30% of each run, Pallas kernels for 0% -> 0%
where the time goes in v1:
time: 98.8 us; the launch traced here: 98 us
  blocking collectives  26.8 us (27%)
  starting transfers between devices  22.6 us (23%)
  other arithmetic  19.6 us (20%)
  local copies, waits for them, and re-layouts  14.1 us (14%)
  waiting for transfers between devices  7.18 us (7%)
  matrix products  6.48 us (7%)
  between operations  1.27 us (1%)
    all_gather x1, blocking collectives, local(): part_keys = lax.all_gather(summary_keys, 'ctx', axis=0, tiled=True)  13.6 us
    all_gather x1, blocking collectives, local(): part_values = lax.all_gather(summary_values, 'ctx', axis=0, tiled=True)  13.2 us
    ppermute x6, starting transfers between devices, from_behind(): return lax.ppermute(value, axis, pairs)  10.1 us
    all_to_all x1, waiting for transfers between devices, local(): lax.all_to_all(served_keys, 'ctx', split_axis=2, concat_axis=2, tiled=True)  7.16 us
    all_to_all x1, starting transfers between devices, local(): lax.all_to_all(jnp.stack(jnp.split(requested, lax.axis_size('ctx'), axis=...  5.27 us
    all_to_all x1, starting transfers between devices, local(): lax.all_to_all(served_keys, 'ctx', split_axis=2, concat_axis=2, tiled=True)  3.66 us
    all_to_all x1, starting transfers between devices, local(): lax.all_to_all(served_values, 'ctx', split_axis=2, concat_axis=2, tiled=T...  3.63 us
    unnamed x39, local copies, waits for them, and re-layouts  3.38 us
  transfers between devices with their start and end apart: 9, of which 1 were waited for; matrix products, arithmetic and copies ran while one was open for 30% of the time, Pallas kernels for 0%

profile of v1, /device:TPU:0, one launch (start us, length us, event | category | flops | bytes accessed | tf_op | source)
XLA Modules:
  0.0 98.0 jit_solution(7257098998032914413)
XLA Ops:
  0.0 1.3 %copy.62 = bf16[1024,192]{1,0:T(8,128)(2,1)S(1)} copy(bf16[1024,192]{0,1:T(8,128)(2,1)} %param.11) | data formatting | bytes 786432 | tf_op args[1]
  1.3 1.1 %copy.60 = bf16[512,192]{1,0:T(8,128)(2,1)S(1)} copy(bf16[512,192]{0,1:T(8,128)(2,1)} %param.13) | data formatting | bytes 393216 | tf_op args[3]
  2.4 0.6 slice_select_fusion.2
  3.0 5.1 %collective-permute-start = (bf16[16,192]{1,0:T(8,128)(2,1)}, bf16[16,192]{1,0:T(8,128)(2,1)}, u32[]{:S(2)}, u32[]{:S(2)}) collective-permute-start(bf16[16,192]{1,0:T(8,128)(2,1)} %get-tuple-element.17), channel_id=1, source_target_pairs={{0,24},{8,0},{16,8},{24,16},{1,25},{9,1},{17,9},{25,17},{2,26},{10... | collective-permute-start | bytes 18440 | tf_op jit(solution)/shard_map/ppermute | solution.py:18
  8.1 0.4 collective-permute-start.1
  8.5 1.3 %slice_select_fusion.3 = (bf16[16,128]{1,0:T(8,128)(2,1)}, bf16[16,128]{1,0:T(8,128)(2,1)}) fusion(bf16[1024,128]{1,0:T(8,128)(2,1)} %param.12, pred[]{:T(512)S(6)} %eq.10, bf16[512,128]{1,0:T(8,128)(2,1)} %param.14), kind=kLoop, calls=%fused_computation.88 | loop fusion | flops 2048 | bytes 16385 | tf_op jit(solution)/shard_map/jit(_where)/select_n | solution.py:70
  9.8 0.4 collective-permute-start.2
  10.4 0.5 broadcast.555
  10.9 1.3 %reduce.11 = s32[16]{0:T(128)S(1)} reduce(s32[1,16]{1,0:T(1,128)} %param.18, s32[]{:T(128)} %broadcast.555), dimensions={0}, to_apply=%param.18.reduce_sub_computation.3 | reduce | bytes 132 | tf_op args[8]
  12.4 0.6 gather_fusion
  13.0 0.2 slice_reduce_fusion.3
  13.3 0.6 pad_add_fusion
  13.8 5.3 %all-to-all-start = ((s32[4,1,4,1]{2,3,1,0:T(1,128)}), s32[4,1,4,1]{2,3,1,0:T(1,128)S(1)}, u32[]{:S(2)}, u32[]{:S(2)}) async-start(s32[4,1,4,1]{2,3,1,0:T(1,128)} %pad_add_fusion), calls=%async_computation | async-start | bytes 4096 | tf_op jit(solution)/shard_map/all_to_all | solution.py:133
  19.1 1.5 %slice_select_fusion = bf16[256,192]{0,1:T(8,128)(2,1)} fusion(bf16[512,192]{0,1:T(8,128)(2,1)S(1)} %copy-done.2, bf16[1024,192]{0,1:T(8,128)(2,1)} %param.11, pred[]{:T(512)S(6)} %eq.11), kind=kLoop, calls=%fused_computation.60 | loop fusion | flops 49152 | bytes 294913 | tf_op jit(solution)/shard_map/jit(_where)/select_n | solution.py:158
  20.7 2.0 %collective-permute-start.4 = (bf16[256,192]{0,1:T(8,128)(2,1)}, bf16[256,192]{0,1:T(8,128)(2,1)}, u32[]{:S(2)}, u32[]{:S(2)}) collective-permute-start(bf16[256,192]{0,1:T(8,128)(2,1)} %slice_select_fusion), channel_id=1, source_target_pairs={{0,8},{8,16},{16,24},{24,0},{1,9},{9,17},{17,25},{25,1},{2,10},{10... | collective-permute-start | bytes 294920 | tf_op jit(solution)/shard_map/ppermute | solution.py:18
  22.7 0.6 multiply_add_fusion
  23.3 0.6 broadcast_add_fusion.1
  23.9 0.6 fusion.31
  24.6 0.6 broadcast_add_fusion
  25.2 0.6 slice_select_fusion.1
  25.8 0.6 reshape.324
  26.6 0.7 add.275
  28.2 0.7 and.99
  28.8 0.6 iota_add_fusion.1
  29.5 0.7 copy.64
  30.2 0.7 copy.79
  30.9 0.6 copy.90
  31.5 0.7 copy.68
  32.6 0.6 gather_fusion.1
  33.1 0.6 gather_fusion.3
  33.7 0.6 gather_fusion.2
  34.3 0.7 gather_fusion.4
  35.1 0.8 broadcast_select_fusion
  35.9 0.7 copy.77
  36.6 3.6 %all-to-all-start.2 = ((bf16[1,4,4,64,128]{4,3,1,0,2:T(8,128)(2,1)}), bf16[1,4,4,64,128]{4,3,1,0,2:T(8,128)(2,1)S(1)}, u32[]{:S(2)}, u32[]{:S(2)}) async-start(bf16[1,4,4,64,128]{4,3,1,0,2:T(8,128)(2,1)} %copy.77), calls=%async_computation.2 | async-start | bytes 524288 | tf_op jit(solution)/shard_map/all_to_all | solution.py:153
  40.2 1.6 %copy_select_fusion = bf16[1,4,4,64,192]{4,3,1,0,2:T(8,128)(2,1)} fusion(bf16[1,4,4,64,192]{4,3,2,1,0:T(8,128)(2,1)S(1)} %bitcast.105, bf16[1,4,4,64,192]{4,3,2,1,0:T(8,128)(2,1)S(1)} %bitcast.104, pred[4,4]{0,1:T(4,128)(4,1)} %bitcast.117), kind=kLoop, calls=%fused_computation.44 | loop fusion | flops 196608 | bytes 1179664 | tf_op jit(solution)/shard_map/jit(_where)/select_n | solution.py:141
  41.8 2.0 %collective-permute-start.5 = (bf16[256,128]{1,0:T(8,128)(2,1)S(1)}, bf16[256,128]{1,0:T(8,128)(2,1)S(1)}, u32[]{:S(2)}, u32[]{:S(2)}) collective-permute-start(bf16[256,128]{1,0:T(8,128)(2,1)S(1)} %copy-done.6), channel_id=1, source_target_pairs={{0,8},{8,16},{16,24},{24,0},{1,9},{9,17},{17,25},{25,1},{2,10},{10... | collective-permute-start | bytes 196616 | tf_op jit(solution)/shard_map/ppermute | solution.py:18
  43.8 0.7 maximum_convert_fusion.2
  44.6 0.7 maximum_convert_fusion.3
  45.4 0.2 multiply_reduce_fusion.2
  45.6 0.1 multiply_reduce_fusion.6
  45.7 13.2 %all_gather.7 = bf16[384,128]{1,0:T(8,128)(2,1)S(1)} all-gather(bf16[96,128]{1,0:T(8,128)(2,1)S(1)} %pad_maximum_fusion.1), channel_id=1, replica_groups=mesh['parts'=1,'ctx'=4,'pb'=4,'row'=2] {'ctx'}, dimensions={0}, use_global_device_ids=true | all-gather | bytes 122880 | tf_op jit(solution)/shard_map/all_gather | solution.py:97
  59.0 0.8 maximum_convert_fusion
  59.8 0.2 fusion.53
  60.0 0.7 maximum_convert_fusion.1
  60.8 0.5 multiply_reduce_fusion
  61.4 0.2 multiply_reduce_fusion.4
  61.7 13.6 %all_gather.6 = bf16[384,192]{1,0:T(8,128)(2,1)S(1)} all-gather(bf16[96,192]{1,0:T(8,128)(2,1)S(1)} %pad_maximum_fusion), channel_id=1, replica_groups=mesh['parts'=1,'ctx'=4,'pb'=4,'row'=2] {'ctx'}, dimensions={0}, use_global_device_ids=true | all-gather | bytes 184320 | tf_op jit(solution)/shard_map/all_gather | solution.py:96
  75.2 0.4 fusion.60
  75.7 0.3 fusion.9
  76.0 0.7 fusion.5
  76.8 3.7 %all-to-all-start.1 = ((bf16[1,4,4,64,192]{4,3,1,0,2:T(8,128)(2,1)}), bf16[1,4,4,64,192]{4,3,1,0,2:T(8,128)(2,1)S(1)}, u32[]{:S(2)}, u32[]{:S(2)}) async-start(bf16[1,4,4,64,192]{4,3,1,0,2:T(8,128)(2,1)} %copy_select_fusion), calls=%async_computation.1 | async-start | bytes 1048576 | tf_op jit(solution)/shard_map/all_to_all | solution.py:152
  80.5 1.7 %fusion.59 = (f32[1024]{0:T(1024)S(1)}, f32[1024,320]{0,1:T(8,128)S(1)}) fusion(bf16[1024,192]{1,0:T(8,128)(2,1)S(1)} %reshape.324, s32[]{:T(128)S(6)} %select_n.217, bf16[256,192]{0,1:T(8,128)(2,1)} %collective-permute-done.4, bf16[512,192]{0,1:T(8,128)(2,1)S(1)} %copy-done.2, s32[1024]{0:T(1024)S(1)} %copy-done.10, s32[1024]{0:T(1024)S(1)} %copy-done.7, ...), kind=kOutput, calls=%fused_computation.143 | convolution fusion | flops 128039936 | bytes 2012420 | tf_op jit(solution)/shard_map/dot_general | solution.py:31
  82.2 0.4 fusion.11
  82.6 0.7 convolution_divide_fusion
  83.4 7.2 %all-to-all-done.1 = bf16[1,4,4,64,192]{4,3,1,0,2:T(8,128)(2,1)S(1)} async-done(((bf16[1,4,4,64,192]{4,3,1,0,2:T(8,128)(2,1)}), bf16[1,4,4,64,192]{4,3,1,0,2:T(8,128)(2,1)S(1)}, u32[]{:S(2)}, u32[]{:S(2)}) %all-to-all-start.1) | async-done | bytes 393248 | tf_op jit(solution)/shard_map/all_to_all | solution.py:152
  90.6 1.2 %fusion = (f32[1024]{0:T(1024)S(1)}, f32[1024,1024]{1,0:T(8,128)S(1)}) fusion(s32[1024]{0:T(1024)S(1)} %copy-done.7, s32[1024]{0:T(1024)S(1)} %copy-done.9, pred[1024]{0:T(1024)(128)(4,1)S(1)} %copy-done.17, bf16[1024,192]{1,0:T(8,128)(2,1)S(1)} %bitcast.113, bf16[1024,192]{1,0:T(8,128)(2,1)S(1)} %reshape.324), kind=kOutput, calls=%fused_computation.8 | convolution fusion | flops 407895040 | bytes 4994048 | tf_op jit(solution)/shard_map/dot_general | solution.py:31
  91.9 1.9 %fusion.52 = f32[1024]{0:T(1024)S(1)} fusion(f32[1024]{0:T(1024)S(1)} %get-tuple-element.34, f32[1024,1024]{1,0:T(8,128)S(1)} %get-tuple-element.35, s32[1024]{0:T(1024)S(1)} %copy-done.7, s32[1024]{0:T(1024)S(1)} %copy-done.9, pred[1024]{0:T(1024)(128)(4,1)S(1)} %copy-done.17), kind=kLoop, calls=%fused_computation.136 | loop fusion | flops 7339008 | bytes 4211712 | tf_op jit(solution)/shard_map/reduce_sum | solution.py:37
  93.8 1.8 %fusion.6 = f32[1024,128]{1,0:T(8,128)S(1)} fusion(bf16[1024,128]{1,0:T(8,128)(2,1)S(1)} %bitcast.114, f32[1024]{0:T(1024)S(1)} %fusion.52, f32[1024,1024]{1,0:T(8,128)S(1)} %get-tuple-element.35, f32[1024]{0:T(1024)S(1)} %get-tuple-element.34, s32[1024]{0:T(1024)S(1)} %copy-done.7, s32[1024]{0:T(1024)S(1)} %copy-done.9, pred[1024]{0:T(1024)(128)(4,1)S(1)} %copy-done.17), kind=kOutput, calls=%fused_computation.20 | convolution fusion | flops 275906560 | bytes 4998144 | tf_op jit(solution)/shard_map/dot_general | solution.py:36
  95.7 0.2 mul.192
  95.9 0.5 copy-done.4
  96.4 0.2 mul.223
  96.6 0.2 mul.234
  96.8 1.3 %fusion.25 = bf16[64,2048]{1,0:T(8,128)(2,1)} fusion(f32[64,2048]{1,0:T(8,128)S(1)} %reshape.332, f32[8,8,16,128]{3,2,1,0:T(8,128)S(1)} %bitcast.108, f32[64,2048]{1,0:T(8,128)S(1)} %reshape.331, f32[8,8,16,128]{3,2,1,0:T(8,128)S(1)} %bitcast.107, f32[64,2048]{1,0:T(8,128)S(1)} %reshape.325, f32[8,8,16,128]{3,2,1,0:T(8,128)S(1)} %bitcast.106), kind=kLoop, calls=%fused_computation.40 | loop fusion | flops 786432 | bytes 3407872 | tf_op jit(solution)/shard_map/convert_element_type | solution.py:193
  (88 shorter events, 2.0 us)
Async XLA Ops:
  0.0 19.1 %copy-start.2 = (bf16[512,192]{0,1:T(8,128)(2,1)S(1)}, bf16[512,192]{0,1:T(8,128)(2,1)}, u32[]{:S(2)}) copy-start(bf16[512,192]{0,1:T(8,128)(2,1)} %param.13) | copy-start | bytes 589828
  0.0 25.2 %copy-start.1 = (bf16[1024,128]{1,0:T(8,128)(2,1)S(1)}, bf16[1024,128]{1,0:T(8,128)(2,1)}, u32[]{:S(2)}) copy-start(bf16[1024,128]{1,0:T(8,128)(2,1)} %param.12) | copy-start | bytes 786436
  0.0 25.2 %copy-start = (bf16[512,128]{1,0:T(8,128)(2,1)S(1)}, bf16[512,128]{1,0:T(8,128)(2,1)}, u32[]{:S(2)}) copy-start(bf16[512,128]{1,0:T(8,128)(2,1)} %param.14) | copy-start | bytes 393220
  0.0 25.8 %copy-start.8 = (f32[32,192]{1,0:T(8,128)S(1)}, f32[32,192]{1,0:T(8,128)}, u32[]{:S(2)}) copy-start(f32[32,192]{1,0:T(8,128)} %param.15) | copy-start | bytes 73732
  0.0 25.8 %copy-start.3 = (bf16[64,3072]{1,0:T(8,128)(2,1)S(1)}, bf16[64,3072]{1,0:T(8,128)(2,1)}, u32[]{:S(2)}) copy-start(bf16[64,3072]{1,0:T(8,128)(2,1)} %param.10) | copy-start | bytes 1179652
  0.0 26.4 %copy-start.13 = (f32[32,128]{1,0:T(8,128)S(1)}, f32[32,128]{1,0:T(8,128)}, u32[]{:S(2)}) copy-start(f32[32,128]{1,0:T(8,128)} %param.16) | copy-start | bytes 49156
  0.0 29.4 %copy-start.14 = (bf16[64,48]{0,1:T(8,128)(2,1)S(1)}, bf16[64,48]{0,1:T(8,128)(2,1)}, u32[]{:S(2)}) copy-start(bf16[64,48]{0,1:T(8,128)(2,1)} %param.17) | copy-start | bytes 18436
  3.0 56.0 %collective-permute-start = (bf16[16,192]{1,0:T(8,128)(2,1)}, bf16[16,192]{1,0:T(8,128)(2,1)}, u32[]{:S(2)}, u32[]{:S(2)}) collective-permute-start(bf16[16,192]{1,0:T(8,128)(2,1)} %get-tuple-element.17), channel_id=1, source_target_pairs={{0,24},{8,0},{16,8},{24,16},{1,25},{9,1},{17,9},{25,17},{2,26},{10... | collective-permute-start | bytes 18440 | tf_op jit(solution)/shard_map/ppermute | solution.py:18
  8.1 51.9 %collective-permute-start.1 = (bf16[16,192]{1,0:T(8,128)(2,1)}, bf16[16,192]{1,0:T(8,128)(2,1)}, u32[]{:S(2)}, u32[]{:S(2)}) collective-permute-start(bf16[16,192]{1,0:T(8,128)(2,1)} %get-tuple-element.18), channel_id=1, source_target_pairs={{0,24},{8,0},{16,8},{24,16},{1,25},{9,1},{17,9},{25,17},{2,26},{10... | collective-permute-start | bytes 18440 | tf_op jit(solution)/shard_map/ppermute | solution.py:18
  9.8 32.0 %collective-permute-start.2 = (bf16[16,128]{1,0:T(8,128)(2,1)}, bf16[16,128]{1,0:T(8,128)(2,1)}, u32[]{:S(2)}, u32[]{:S(2)}) collective-permute-start(bf16[16,128]{1,0:T(8,128)(2,1)} %get-tuple-element.19), channel_id=1, source_target_pairs={{0,24},{8,0},{16,8},{24,16},{1,25},{9,1},{17,9},{25,17},{2,26},{10... | collective-permute-start | bytes 12296 | tf_op jit(solution)/shard_map/ppermute | solution.py:18
  10.3 34.3 %collective-permute-start.3 = (bf16[16,128]{1,0:T(8,128)(2,1)}, bf16[16,128]{1,0:T(8,128)(2,1)}, u32[]{:S(2)}, u32[]{:S(2)}) collective-permute-start(bf16[16,128]{1,0:T(8,128)(2,1)} %get-tuple-element.20), channel_id=1, source_target_pairs={{0,24},{8,0},{16,8},{24,16},{1,25},{9,1},{17,9},{25,17},{2,26},{10... | collective-permute-start | bytes 12296 | tf_op jit(solution)/shard_map/ppermute | solution.py:18
  13.8 17.0 %all-to-all-start = ((s32[4,1,4,1]{2,3,1,0:T(1,128)}), s32[4,1,4,1]{2,3,1,0:T(1,128)S(1)}, u32[]{:S(2)}, u32[]{:S(2)}) async-start(s32[4,1,4,1]{2,3,1,0:T(1,128)} %pad_add_fusion), calls=%async_computation | async-start | bytes 4096 | tf_op jit(solution)/shard_map/all_to_all | solution.py:133
  20.7 59.9 %collective-permute-start.4 = (bf16[256,192]{0,1:T(8,128)(2,1)}, bf16[256,192]{0,1:T(8,128)(2,1)}, u32[]{:S(2)}, u32[]{:S(2)}) collective-permute-start(bf16[256,192]{0,1:T(8,128)(2,1)} %slice_select_fusion), channel_id=1, source_target_pairs={{0,8},{8,16},{16,24},{24,0},{1,9},{9,17},{17,25},{25,1},{2,10},{10... | collective-permute-start | bytes 294920 | tf_op jit(solution)/shard_map/ppermute | solution.py:18
  32.6 1.8 %copy-start.12 = (s32[1024]{0:T(1024)}, s32[1024]{0:T(1024)S(1)}, u32[]{:S(2)}) copy-start(s32[1024]{0:T(1024)S(1)} %pad_clamp_fusion) | copy-start | bytes 12292
  35.9 5.9 %copy-start.6 = (bf16[256,128]{1,0:T(8,128)(2,1)S(1)}, bf16[256,128]{1,0:T(8,128)(2,1)}, u32[]{:S(2)}) copy-start(bf16[256,128]{1,0:T(8,128)(2,1)} %slice_select_fusion.1) | copy-start | bytes 196612
  36.6 40.2 %all-to-all-start.2 = ((bf16[1,4,4,64,128]{4,3,1,0,2:T(8,128)(2,1)}), bf16[1,4,4,64,128]{4,3,1,0,2:T(8,128)(2,1)S(1)}, u32[]{:S(2)}, u32[]{:S(2)}) async-start(bf16[1,4,4,64,128]{4,3,1,0,2:T(8,128)(2,1)} %copy.77), calls=%async_computation.2 | async-start | bytes 524288 | tf_op jit(solution)/shard_map/all_to_all | solution.py:153
  41.8 40.8 %collective-permute-start.5 = (bf16[256,128]{1,0:T(8,128)(2,1)S(1)}, bf16[256,128]{1,0:T(8,128)(2,1)S(1)}, u32[]{:S(2)}, u32[]{:S(2)}) collective-permute-start(bf16[256,128]{1,0:T(8,128)(2,1)S(1)} %copy-done.6), channel_id=1, source_target_pairs={{0,8},{8,16},{16,24},{24,0},{1,9},{9,17},{17,25},{25,1},{2,10},{10... | collective-permute-start | bytes 196616 | tf_op jit(solution)/shard_map/ppermute | solution.py:18
  60.8 14.4 %copy-start.11 = (s32[1024]{0:T(1024)S(1)}, s32[1024]{0:T(1024)}, u32[]{:S(2)}) copy-start(s32[1024]{0:T(1024)} %broadcast_add_fusion.1) | copy-start | bytes 12292
  60.8 14.4 %copy-start.16 = (s32[384]{0:T(512)S(1)}, s32[384]{0:T(512)}, u32[]{:S(2)}) copy-start(s32[384]{0:T(512)} %multiply_add_fusion) | copy-start | bytes 4612
  76.7 3.8 %copy-start.7 = (s32[1024]{0:T(1024)S(1)}, s32[1024]{0:T(1024)}, u32[]{:S(2)}) copy-start(s32[1024]{0:T(1024)} %fusion.31) | copy-start | bytes 12292
  76.7 3.8 %copy-start.10 = (s32[1024]{0:T(1024)S(1)}, s32[1024]{0:T(1024)}, u32[]{:S(2)}) copy-start(s32[1024]{0:T(1024)} %broadcast_add_fusion) | copy-start | bytes 12292
  76.7 3.8 %copy-start.15 = (s32[320]{0:T(512)S(1)}, s32[320]{0:T(512)}, u32[]{:S(2)}) copy-start(s32[320]{0:T(512)} %iota_add_fusion.1) | copy-start | bytes 3844
  76.8 13.7 %all-to-all-start.1 = ((bf16[1,4,4,64,192]{4,3,1,0,2:T(8,128)(2,1)}), bf16[1,4,4,64,192]{4,3,1,0,2:T(8,128)(2,1)S(1)}, u32[]{:S(2)}, u32[]{:S(2)}) async-start(bf16[1,4,4,64,192]{4,3,1,0,2:T(8,128)(2,1)} %copy_select_fusion), calls=%async_computation.1 | async-start | bytes 1048576 | tf_op jit(solution)/shard_map/all_to_all | solution.py:152
  83.3 7.3 %copy-start.9 = (s32[1024]{0:T(1024)S(1)}, s32[1024]{0:T(1024)}, u32[]{:S(2)}) copy-start(s32[1024]{0:T(1024)} %add.275) | copy-start | bytes 12292
  83.3 7.3 %copy-start.17 = (pred[1024]{0:T(1024)(128)(4,1)S(1)}, pred[1024]{0:T(1024)(128)(4,1)}, u32[]{:S(2)}) copy-start(pred[1024]{0:T(1024)(128)(4,1)} %and.99) | copy-start | bytes 3076
  95.6 0.8 copy-start.4
  95.6 0.9 copy-start.5
